TPU v7x, 32 devices: a whole 2x2x4 slice. The times are simulated.
32 devices in a mesh: dp: 8 (over z, x), tensor: 4 (over y, core).
Axes of the slice: x: 2, y: 2, z: 4, core: 2. Of those that a mesh axis runs over, the one named last changes fastest.
Arguments:
- gate_preactivation: bfloat16 [128, 28672], P('dp', 'tensor'), may hold values from -6 to 6
- up_preactivation: bfloat16 [128, 28672], P('dp', 'tensor'), may hold values from -6 to 6
- cotangent: bfloat16 [128, 8192], P('dp'), may hold values from -0.5 to 0.5
- down_weight: bfloat16 [28672, 8192], P('tensor', 'dp'), may hold values from -0.03125 to 0.03125
- lowrank_factor_first: bfloat16 [28672, 64], P('tensor'), may hold values from -0.03125 to 0.03125
- lowrank_factor_second: bfloat16 [64, 8192], replicated, may hold values from -0.75 to 0.75
- sparse_block_values: bfloat16 [8, 4, 2, 128, 128], P('dp', 'tensor'), may hold values from -0.5 to 0.5
- slot_block_rows: int32 [8, 4, 2], P(None, 'tensor'), may hold values from 0 to 55, as said below
- slot_block_columns: int32 [8, 4, 2], P(None, 'tensor'), may hold values from 0 to 7
- owner_slot_counts: int32 [8, 4], P(None, 'tensor'), may hold values from 1 to 2, as said below
Outputs:
- mixed: bfloat16 [128, 8192], P('tensor', 'dp')
- grad_a: float32 [28672, 64], P('tensor')
- grad_b: float32 [64, 8192], P(None, 'dp')
- grad_blocks: float32 [8, 4, 2, 128, 128], P('dp', 'tensor')
Inputs may be any that keep to these rules, and one draw needn't show every extreme that they name: `slot_block_rows`: the 2 slots of one owner name different blocks. `owner_slot_counts`: some owner has exactly 2 live slots.
All inputs are finite; a program needn't handle non-finite values.
Results may differ from a plain program's by a relative error of at most 0.0049.
Values may be sent and summed in bfloat16 or wider, within the bound.
A program may use at most 128 MiB of HBM per device.

v0:
```python
import jax
import jax.numpy as jnp
from jax import lax
from jax.sharding import PartitionSpec as P


def shards(
    gate_preactivation,
    up_preactivation,
    cotangent,
    down_weight,
    lowrank_factor_first,
    lowrank_factor_second,
    sparse_block_values,
    slot_block_rows,
    slot_block_columns,
    owner_slot_counts,
):
    n_dp = lax.axis_size("dp")
    data_parallel_index = lax.axis_index("dp")
    tok_local = gate_preactivation.shape[0]
    quarter = gate_preactivation.shape[1]
    column_offset = down_weight.shape[1]
    side = sparse_block_values.shape[-1]
    slots = sparse_block_values.shape[2]
    per_row = quarter // side
    per_col = column_offset // side
    hidden_activation = (
        jax.nn.silu(gate_preactivation.astype(jnp.float32)) * up_preactivation.astype(jnp.float32)
    ).astype(jnp.bfloat16)
    hidden_gathered = lax.all_gather(hidden_activation, "dp", axis=0, tiled=True)
    tok_all = hidden_gathered.shape[0]
    rows_all = slot_block_rows[:, 0, :]
    cols_all = slot_block_columns[:, 0, :]
    live_all = (
        jnp.arange(slots, dtype=jnp.int32)[None, :] < owner_slot_counts[:, 0][:, None]
    ).astype(jnp.float32)
    own_rows = lax.dynamic_index_in_dim(rows_all, data_parallel_index, 0, keepdims=False)
    own_cols = lax.dynamic_index_in_dim(cols_all, data_parallel_index, 0, keepdims=False)
    own_live = lax.dynamic_index_in_dim(live_all, data_parallel_index, 0, keepdims=False)
    factor_b_window = lax.dynamic_slice_in_dim(
        lowrank_factor_second, data_parallel_index * column_offset, column_offset, 1
    ).astype(jnp.float32)
    col_pick = (own_cols[:, None] == jnp.arange(per_col, dtype=jnp.int32)[None, :]).astype(
        jnp.float32
    ) * own_live[:, None]
    blocks = sparse_block_values[0, 0]
    owned_hidden = jnp.stack(
        [
            lax.dynamic_slice_in_dim(hidden_gathered, own_rows[slot] * side, side, 1)
            for slot in range(slots)
        ],
        axis=1,
    )
    total = jnp.dot(hidden_gathered, down_weight, preferred_element_type=jnp.float32)
    lowrank_token_rows = jnp.dot(
        hidden_gathered, lowrank_factor_first, preferred_element_type=jnp.float32
    )
    total = total + jnp.dot(lowrank_token_rows, factor_b_window, precision=lax.Precision.HIGHEST)
    local = jnp.einsum("tkc,kcd->tkd", owned_hidden, blocks, preferred_element_type=jnp.float32)
    spread = jnp.einsum("tkd,kn->tnd", local, col_pick, precision=lax.Precision.HIGHEST)
    summed = lax.psum_scatter(
        total
        + spread.reshape(
            tok_all // lax.axis_size("tensor") * lax.axis_size("tensor"), column_offset
        ),
        "tensor",
        scatter_dimension=0,
        tiled=True,
    )
    mixed = summed.astype(jnp.bfloat16)
    cotangent_lowrank = lax.dot_general(
        cotangent,
        lowrank_factor_second,
        (((1,), (1,)), ((), ())),
        preferred_element_type=jnp.float32,
    ).astype(jnp.bfloat16)
    lowrank_local_part = jnp.dot(
        hidden_activation, lowrank_factor_first, preferred_element_type=jnp.float32
    )
    part_b = lax.dot_general(
        lowrank_local_part,
        cotangent.astype(jnp.float32),
        (((0,), (0,)), ((), ())),
        precision=lax.Precision.HIGHEST,
    )
    shard_b = lax.psum_scatter(part_b, "dp", scatter_dimension=1, tiled=True)
    grad_b = lax.psum(shard_b, "tensor")
    cot_all = lax.all_gather(cotangent_lowrank, "dp", axis=0, tiled=True)
    grad_a = lax.dot_general(
        hidden_gathered, cot_all, (((0,), (0,)), ((), ())), preferred_element_type=jnp.float32
    )
    picked_h = jnp.take(
        hidden_activation.reshape(tok_local, per_row, side), rows_all.reshape(-1), axis=1
    )
    picked_h = picked_h.reshape(tok_local, n_dp, slots, side)
    pick_all = (cols_all[:, :, None] == jnp.arange(per_col, dtype=jnp.int32)[None, None, :]).astype(
        jnp.bfloat16
    )
    cot_split = cotangent.reshape(tok_local, n_dp, per_col, side)
    picked_c = jnp.einsum(
        "tond,okn->tokd", cot_split, pick_all, preferred_element_type=jnp.float32
    ).astype(jnp.bfloat16)
    partial_value = jnp.einsum(
        "tokc,tokd->okcd", picked_h, picked_c, preferred_element_type=jnp.float32
    )
    partial_value = partial_value * live_all[:, :, None, None]
    owned = lax.psum_scatter(partial_value, "dp", scatter_dimension=0, tiled=True)
    grad_blocks = owned[:, None]
    return (mixed, grad_a, grad_b, grad_blocks)


def solution(mesh):
    return jax.shard_map(
        shards,
        mesh=mesh,
        in_specs=(
            P("dp", "tensor"),
            P("dp", "tensor"),
            P("dp", None),
            P("tensor", "dp"),
            P("tensor", None),
            P(),
            P("dp", "tensor", None, None, None),
            P(None, "tensor", None),
            P(None, "tensor", None),
            P(None, "tensor"),
        ),
        out_specs=(
            P("tensor", "dp"),
            P("tensor", None),
            P(None, "dp"),
            P("dp", "tensor", None, None, None),
        ),
        check_vma=False,
    )
```

profile of v0, /device:TPU:0, one launch (start us, length us, event | category | flops | bytes accessed | tf_op | source)
XLA Modules:
  0.0 262.6 jit_solution(11107851190371426285)
XLA Ops:
  7.2 0.0 copy-start
  7.2 0.0 copy-start.3
  7.2 0.0 all-gather.2.cloned.1.call-start
  7.2 2.0 fusion.6
  9.2 0.0 all-gather.2.cloned.1.call-update
  9.2 0.0 reduce-scatter.6.cloned.1.call-start
  9.3 1.6 fusion.41
  10.9 0.0 copy-start.6
  11.0 2.4 fusion.42
  13.3 0.0 reduce-scatter.6.cloned.1.call-update
  13.4 0.0 reduce-scatter.4.cloned.1.call-start
  13.4 0.0 copy-done.5
  13.4 0.1 constant_dynamic-slice_fusion
  13.5 0.5 fusion.37
  15.3 0.1 copy.23
  15.4 0.2 fusion.25
  15.6 0.1 copy.22
  15.7 0.1 copy.25
  15.8 0.1 reshape_squeeze.6
  15.9 0.8 copy.31
  16.6 0.1 fusion.23
  16.7 43.1 %all-gather.2.cloned.1.call-done = bf16[128,7168]{1,0:T(8,128)(2,1)} async-done(((bf16[16,7168]{1,0:T(8,128)(2,1)}), bf16[128,7168]{1,0:T(8,128)(2,1)}) %all-gather.2.cloned.1.call-update) | async-done | bytes 1835024 | tf_op jit(solution)/shard_map/all_gather | solution.py:31
  59.8 0.8 dynamic-slice_bitcast_fusion.1
  60.5 0.0 copy-done.4
  60.5 0.1 convolution_bitcast_fusion
  60.7 0.8 fusion.8
  61.5 2.5 fusion.39
  64.0 7.2 %fusion.38 = f32[128,1024]{1,0:T(8,128)S(1)} fusion(bf16[128,7168]{1,0:T(8,128)(2,1)S(1)} %copy-done.1, bf16[7168,1024]{1,0:T(8,128)(2,1)} %param.13), kind=kOutput, calls=%fused_computation.57 | convolution fusion | flops 1879048192 | bytes 17039360 | tf_op jit(solution)/shard_map/dot_general | solution.py:55
  71.2 0.0 copy-start.2
  71.2 1.4 fusion
  72.6 0.0 reduce-scatter.4.cloned.1.call-update
  72.6 0.0 reduce-scatter.8.cloned.1.call-start
  72.7 0.7 copy_bitcast_fusion
  73.4 1.5 gather_fusion
  74.9 1.2 fusion.1
  76.2 1.4 convolution_multiply_fusion
  77.6 0.0 reduce-scatter.8.cloned.1.call-update
  77.6 0.0 all-reduce.2.cloned.1.call-start
  77.7 0.4 convolution_convert_fusion.1
  78.0 30.4 %all_gather.7 = bf16[128,64]{1,0:T(8,128)(2,1)S(1)} all-gather(bf16[16,64]{1,0:T(8,128)(2,1)S(1)} %convolution_convert_fusion.1), channel_id=1, replica_groups=mesh['dp'=8,'tensor'=4] {'dp'}, dimensions={0}, use_global_device_ids=true | all-gather | bytes 18432 | tf_op jit(solution)/shard_map/all_gather | solution.py:89
  108.5 21.9 %reduce-scatter.6.cloned.1.call-done = f32[64,1024]{1,0:T(8,128)} async-done(((f32[64,8192]{1,0:T(8,128)}), f32[64,1024]{1,0:T(8,128)}) %reduce-scatter.6.cloned.1.call-update) | async-done | bytes 262160 | tf_op jit(solution)/shard_map/reduce_scatter | solution.py:87
  130.4 0.0 all-reduce.2.cloned.1.call-update
  130.5 1.7 fusion.40
  132.1 21.5 %reduce-scatter.4.cloned.1.call-done = f32[32,1024]{1,0:T(8,128)} async-done(((f32[128,1024]{1,0:T(8,128)}), f32[32,1024]{1,0:T(8,128)}) %reduce-scatter.4.cloned.1.call-update) | async-done | bytes 131088 | tf_op jit(solution)/shard_map/reduce_scatter | solution.py:62
  153.6 1.5 convert_element_type.36
  155.2 66.0 %reduce-scatter.8.cloned.1.call-done = f32[1,2,128,128]{3,2,1,0:T(8,128)} async-done(((f32[8,2,128,128]{3,2,1,0:T(8,128)}), f32[1,2,128,128]{3,2,1,0:T(8,128)}) %reduce-scatter.8.cloned.1.call-update) | async-done | bytes 131088 | tf_op jit(solution)/shard_map/reduce_scatter | solution.py:108
  221.2 33.2 %all-reduce.2.cloned.1.call-done = f32[64,1024]{1,0:T(8,128)} async-done(((f32[64,1024]{1,0:T(8,128)}), f32[64,1024]{1,0:T(8,128)}) %all-reduce.2.cloned.1.call-update) | async-done | bytes 262160 | tf_op jit(solution)/shard_map/psum | solution.py:88
  254.4 1.7 copy.41
  (14 shorter events, 0.0 us)
Async XLA Ops:
  7.2 64.1 %copy-start = (bf16[64,8192]{1,0:T(8,128)(2,1)S(1)}, bf16[64,8192]{1,0:T(8,128)(2,1)}, u32[]{:S(2)}) copy-start(bf16[64,8192]{1,0:T(8,128)(2,1)} %param.15) | copy-start | bytes 3145732
  7.2 3.8 %copy-start.3 = (bf16[16,8192]{1,0:T(8,128)(2,1)S(1)}, bf16[16,8192]{1,0:T(8,128)(2,1)}, u32[]{:S(2)}) copy-start(bf16[16,8192]{1,0:T(8,128)(2,1)} %param.12) | copy-start | bytes 786436
  7.2 52.6 %all-gather.2.cloned.1.call-start = ((), (), s32[]{:S(2)}) async-start(), calls=%async_computation.3 | async-start | bytes 2064384 | tf_op jit(solution)/shard_map/all_gather | solution.py:31
  9.2 121.2 %reduce-scatter.6.cloned.1.call-start = ((), (), s32[]{:S(2)}) async-start(), calls=%async_computation.5 | async-start | bytes 2359296 | tf_op jit(solution)/shard_map/reduce_scatter | solution.py:87
  10.9 2.5 copy-start.5
  10.9 4.5 %copy-start.6 = (s32[8,1,2]{0,2,1:T(2,128)S(1)}, s32[8,1,2]{0,2,1:T(2,128)}, u32[]{:S(2)}) copy-start(s32[8,1,2]{0,2,1:T(2,128)} %param.18) | copy-start | bytes 196
  13.3 3.3 %copy-start.7 = (s32[8,1]{0,1:T(1,128)S(1)}, s32[8,1]{0,1:T(1,128)}, u32[]{:S(2)}) copy-start(s32[8,1]{0,1:T(1,128)} %param.19) | copy-start | bytes 100
  13.3 47.2 %copy-start.4 = (bf16[1,1,2,128,128]{4,3,2,1,0:T(8,128)(2,1)S(1)}, bf16[1,1,2,128,128]{4,3,2,1,0:T(8,128)(2,1)}, u32[]{:S(2)}) copy-start(bf16[1,1,2,128,128]{4,3,2,1,0:T(8,128)(2,1)} %param.16) | copy-start | bytes 196612
  13.4 140.3 %reduce-scatter.4.cloned.1.call-start = ((), (), s32[]{:S(2)}) async-start(), calls=%async_computation.4 | async-start | bytes 655360 | tf_op jit(solution)/shard_map/reduce_scatter | solution.py:62
  60.5 3.4 %copy-start.1 = (bf16[128,7168]{1,0:T(8,128)(2,1)S(1)}, bf16[128,7168]{1,0:T(8,128)(2,1)}, u32[]{:S(2)}) copy-start(bf16[128,7168]{1,0:T(8,128)(2,1)} %all-gather.2.cloned.1.call-done) | copy-start | bytes 5505028
  71.2 1.5 copy-start.2
  72.6 148.6 %reduce-scatter.8.cloned.1.call-start = ((), (), s32[]{:S(2)}) async-start(), calls=%async_computation.7 | async-start | bytes 1179648 | tf_op jit(solution)/shard_map/reduce_scatter | solution.py:108
  77.6 176.8 %all-reduce.2.cloned.1.call-start = ((), (), s32[]{:S(2)}) async-start(), calls=%async_computation.6 | async-start | bytes 524288 | tf_op jit(solution)/shard_map/psum | solution.py:88
Sparse Core Ops, SparseCore 0:
  10.8 48.9 all-gather.1
  63.3 67.1 reduce-scatter.5
  132.9 20.6 reduce-scatter.3
  157.8 63.3 reduce-scatter.7
  223.4 30.9 all-reduce.1
where the time goes:
time: 263 us
  waiting for transfers between devices  186 us (71%)
  blocking collectives  30.4 us (12%)
  matrix products  20.7 us (8%)
  between operations  15.2 us (6%)
  local copies, waits for them, and re-layouts  6.63 us (3%)
  other arithmetic  3.61 us (1%)
    reduce_scatter x1, waiting for transfers between devices, shards(): lax.psum_scatter(partial_value, 'dp', scatter_dimension=0, tiled=True)  66 us
    all_gather x1, waiting for transfers between devices, shards(): lax.all_gather(hidden_activation, 'dp', axis=0, tiled=True)  43.1 us
    psum x1, waiting for transfers between devices, shards(): grad_b = lax.psum(shard_b, 'tensor')  33.2 us
    all_gather x1, blocking collectives, shards(): cot_all = lax.all_gather(cotangent_lowrank, 'dp', axis=0, tiled=True)  30.4 us
    reduce_scatter x1, waiting for transfers between devices, shards(): shard_b = lax.psum_scatter(part_b, 'dp', scatter_dimension=1, tiled=True)  21.9 us
    reduce_scatter x1, waiting for transfers between devices, shards(): lax.psum_scatter(total + spread.reshape(tok_all // lax.axis_size('tensor'...  21.5 us
    dot_general x1, matrix products, shards(): jnp.dot(hidden_gathered, down_weight, preferred_element_type=jnp.float32)  7.23 us
  transfers between devices with their start and end apart: 5, of which 5 were waited for; matrix products, arithmetic and copies ran while one was open for 10% of the time, Pallas kernels for 0%

commit v1 on v0

v1 whole, which is shorter than its diff:
```python
import jax
import jax.numpy as jnp
from jax import lax
from jax.sharding import PartitionSpec as P


def shards(gate, up, cotangent, down_weight, factor_a, factor_b, blocks, slot_rows, slot_cols, counts):
    f32, bf16 = jnp.float32, jnp.bfloat16
    n_dp = lax.axis_size("dp")
    me = lax.axis_index("dp")
    tok_local, quarter = gate.shape
    width = down_weight.shape[1]
    rank = factor_a.shape[1]
    side = blocks.shape[-1]
    slots = blocks.shape[2]
    per_col = width // side
    hidden = (jax.nn.silu(gate.astype(f32)) * up.astype(f32)).astype(bf16)
    cot_low = lax.dot_general(
        cotangent, factor_b, (((1,), (1,)), ((), ())), preferred_element_type=f32
    ).astype(bf16)
    packed = jnp.concatenate([hidden, cot_low, jnp.zeros_like(cot_low)], axis=1)
    packed_all = lax.all_gather(packed, "dp", axis=0, tiled=True)
    hidden_all = packed_all[:, :quarter]
    cot_low_all = packed_all[:, quarter : quarter + rank]
    tok_all = tok_local * n_dp
    cot_cols = lax.all_to_all(
        cotangent.reshape(tok_local, n_dp, width), "dp", split_axis=1, concat_axis=0, tiled=True
    ).reshape(tok_all, width)
    rows = lax.dynamic_index_in_dim(slot_rows[:, 0, :], me, 0, keepdims=False)
    cols = lax.dynamic_index_in_dim(slot_cols[:, 0, :], me, 0, keepdims=False)
    live = jnp.arange(slots, dtype=jnp.int32) < lax.dynamic_index_in_dim(
        counts[:, 0], me, 0, keepdims=False
    )
    b_window = lax.dynamic_slice_in_dim(factor_b, me * width, width, 1).astype(f32)
    low = jnp.dot(hidden_all, factor_a, preferred_element_type=f32)
    total = jnp.dot(hidden_all, down_weight, preferred_element_type=f32)
    total = total + jnp.dot(low, b_window, precision=lax.Precision.HIGHEST)
    owned_h = [
        lax.dynamic_slice_in_dim(hidden_all, rows[s] * side, side, 1) for s in range(slots)
    ]
    owned_c = [
        lax.dynamic_slice_in_dim(cot_cols, cols[s] * side, side, 1) for s in range(slots)
    ]
    lanes = jnp.arange(per_col, dtype=jnp.int32)
    for s in range(slots):
        piece = jnp.dot(owned_h[s], blocks[0, 0, s], preferred_element_type=f32)
        pick = (lanes == cols[s]) & live[s]
        total = total + jnp.where(
            pick[None, :, None], piece[:, None, :], 0.0
        ).reshape(tok_all, width)
    mixed = lax.psum_scatter(total, "tensor", scatter_dimension=0, tiled=True).astype(bf16)
    low_parts = lax.all_gather(low, "tensor", axis=0)
    low_sum = jnp.sum(low_parts, axis=0)
    grad_b = lax.dot_general(
        low_sum,
        cot_cols.astype(f32),
        (((0,), (0,)), ((), ())),
        precision=lax.Precision.HIGHEST,
    )
    grad_a = lax.dot_general(
        hidden_all, cot_low_all, (((0,), (0,)), ((), ())), preferred_element_type=f32
    )
    grad_blocks = jnp.stack(
        [
            jnp.where(
                live[s],
                lax.dot_general(
                    owned_h[s],
                    owned_c[s],
                    (((0,), (0,)), ((), ())),
                    preferred_element_type=f32,
                ),
                0.0,
            )
            for s in range(slots)
        ]
    )[None, None]
    return (mixed, grad_a, grad_b, grad_blocks)


def solution(mesh):
    return jax.shard_map(
        shards,
        mesh=mesh,
        in_specs=(
            P("dp", "tensor"),
            P("dp", "tensor"),
            P("dp", None),
            P("tensor", "dp"),
            P("tensor", None),
            P(),
            P("dp", "tensor", None, None, None),
            P(None, "tensor", None),
            P(None, "tensor", None),
            P(None, "tensor"),
        ),
        out_specs=(
            P("tensor", "dp"),
            P("tensor", None),
            P(None, "dp"),
            P("dp", "tensor", None, None, None),
        ),
        check_vma=False,
    )
```

time: 263 us -> 105 us (0.40)
  waiting for transfers between devices: 186 us -> 44.1 us
  blocking collectives: 30.4 us -> 5.43 us
  starting transfers between devices: 0.21 us -> 7.33 us
  matrix products: 20.7 us -> 16.8 us
  other arithmetic: 3.61 us -> 6.64 us
    reduce_scatter x3 -> x1, waiting for transfers between devices: 109 us -> 7.61 us  [shards(): lax.psum_scatter(total, 'tensor', scatter_dimension=0, tiled=True)]
    psum x1 -> x0, waiting for transfers between devices: 33.2 us -> none  [shards(): grad_b = lax.psum(shard_b, 'tensor')]
    all_gather x1, blocking collectives: 30.4 us -> 5.43 us  [shards(): low_parts = lax.all_gather(low, 'tensor', axis=0)]
    all_to_all x0 -> x1, starting transfers between devices: none -> 7.25 us  [shards(): lax.all_to_all(cotangent.reshape(tok_local, n_dp, width), 'dp', split_axi...]
    all_gather x1, waiting for transfers between devices: 43.1 us -> 36.5 us  [shards(): packed_all = lax.all_gather(packed, 'dp', axis=0, tiled=True)]
    dot_general x11 -> x10, matrix products: 20.7 us -> 16.8 us  [the longest x1 7.23 us: shards(): total = jnp.dot(hidden_all, down_weight, preferred_element_type=f32)]
    slice x1 -> x4, local copies, waits for them, and re-layouts: 0.52 us -> 3.39 us  [the longest x1 1.77 us: shards(): hidden_all = packed_all[:, :quarter]]
  transfers between devices with their start and end apart: 5 -> 3, of which waited for: 5 -> 2; matrix products, arithmetic and copies ran while one was open for 10% -> 23% of each run, Pallas kernels for 0% -> 0%
where the time goes in v1:
time: 105 us; the launch traced here: 104 us
  waiting for transfers between devices  44.1 us (42%)
  matrix products  16.8 us (16%)
  between operations  16.7 us (16%)
  starting transfers between devices  7.33 us (7%)
  local copies, waits for them, and re-layouts  7.04 us (7%)
  other arithmetic  6.64 us (6%)
  blocking collectives  5.43 us (5%)
    all_gather x1, waiting for transfers between devices, shards(): packed_all = lax.all_gather(packed, 'dp', axis=0, tiled=True)  36.5 us
    reduce_scatter x1, waiting for transfers between devices, shards(): lax.psum_scatter(total, 'tensor', scatter_dimension=0, tiled=True)  7.61 us
    all_to_all x1, starting transfers between devices, shards(): lax.all_to_all(cotangent.reshape(tok_local, n_dp, width), 'dp', split_axi...  7.25 us
    dot_general x1, matrix products, shards(): total = jnp.dot(hidden_all, down_weight, preferred_element_type=f32)  7.23 us
    all_gather x1, blocking collectives, shards(): low_parts = lax.all_gather(low, 'tensor', axis=0)  5.43 us
    dot_general x2, matrix products, shards(): lax.dot_general(owned_h[s], owned_c[s], (((0,), (0,)), ((), ())), preferr...  3.19 us
    and x2, other arithmetic, shards(): pick = (lanes == cols[s]) & live[s]  2.46 us
  transfers between devices with their start and end apart: 3, of which 2 were waited for; matrix products, arithmetic and copies ran while one was open for 23% of the time, Pallas kernels for 0%

profile of v1, /device:TPU:0, one launch (start us, length us, event | category | flops | bytes accessed | tf_op | source)
XLA Modules:
  0.0 104.0 jit_solution(18101052415162952382)
XLA Ops:
  7.2 0.0 copy-start
  7.2 0.0 copy-start.3
  7.2 0.0 copy-start.5
  7.2 0.0 copy-start.6
  7.2 0.0 copy-start.8
  7.2 0.0 all-gather.3.cloned.1.call-start
  7.3 1.3 %fusion.8 = bf16[16,7168]{1,0:T(8,128)(2,1)S(1)} fusion(bf16[16,7168]{1,0:T(8,128)(2,1)} %param.11, bf16[16,7168]{1,0:T(8,128)(2,1)} %param.10), kind=kLoop, calls=%fused_computation.16 | loop fusion | flops 917504 | bytes 688128 | tf_op jit(solution)/shard_map/convert_element_type | solution.py:17
  8.5 0.1 copy-done
  8.6 1.3 %convolution_convert_fusion = bf16[16,64]{1,0:T(8,128)(2,1)S(1)} fusion(bf16[16,8192]{1,0:T(8,128)(2,1)} %param.12, bf16[64,8192]{1,0:T(8,128)(2,1)S(1)} %copy-done), kind=kOutput, calls=%fused_computation.7 | convolution fusion | flops 16778240 | bytes 1312768 | tf_op jit(solution)/shard_map/dot_general | solution.py:18
  9.9 0.8 concatenate.3
  10.7 0.0 all-gather.3.cloned.1.call-update
  10.8 0.0 copy-done.3
  10.8 0.7 copy.22
  11.5 7.3 %all-to-all-start = ((bf16[16,8,1024]{2,0,1:T(8,128)(2,1)}), bf16[16,8,1024]{2,0,1:T(8,128)(2,1)S(1)}, u32[]{:S(2)}, u32[]{:S(2)}) async-start(bf16[16,8,1024]{2,0,1:T(8,128)(2,1)} %bitcast.50), calls=%async_computation.1 | async-start | bytes 524288 | tf_op jit(solution)/shard_map/all_to_all | solution.py:26
  18.7 0.0 reduce-scatter.2.cloned.1.call-start
  18.8 0.0 copy-done.5
  18.8 0.0 copy-done.6
  18.8 0.1 constant_dynamic-slice_fusion
  18.9 0.5 fusion.35
  20.7 0.6 constant_dynamic-slice_fusion.1
  21.3 0.6 iota_compare_fusion
  22.0 0.5 fusion.34
  22.5 0.6 fusion.36
  23.1 1.2 %compare_and_fusion = pred[8]{0:T(512)(128)(4,1)S(1)} fusion(pred[]{:T(512)} %bitcast.7, s32[]{:T(128)} %bitcast.6), kind=kLoop, calls=%fused_computation.42 | loop fusion | flops 16 | bytes 13 | tf_op jit(solution)/shard_map/and | solution.py:47
  24.3 1.3 %compare_and_fusion.1 = pred[8]{0:T(512)(128)(4,1)S(1)} fusion(pred[]{:T(512)} %bitcast.2, s32[]{:T(128)} %bitcast), kind=kLoop, calls=%fused_computation.43 | loop fusion | flops 16 | bytes 13 | tf_op jit(solution)/shard_map/and | solution.py:47
  25.5 0.1 broadcast_bitcast_fusion
  25.6 0.1 broadcast_bitcast_fusion.1
  25.7 36.5 %all-gather.3.cloned.1.call-done = bf16[128,7296]{1,0:T(8,128)(2,1)} async-done(((bf16[16,7296]{1,0:T(8,128)(2,1)}), bf16[128,7296]{1,0:T(8,128)(2,1)}) %all-gather.3.cloned.1.call-update) | async-done | bytes 1867792 | tf_op jit(solution)/shard_map/all_gather | solution.py:22
  62.2 1.8 %slice.48 = bf16[128,7168]{1,0:T(8,128)(2,1)S(1)} slice(bf16[128,7296]{1,0:T(8,128)(2,1)} %all-gather.3.cloned.1.call-done), slice={[0:128], [0:7168]} | slice | bytes 3670016 | tf_op jit(solution)/shard_map/slice | solution.py:23
  63.9 0.0 copy-done.4
  63.9 0.0 copy-start.2
  64.0 0.1 fusion.14
  64.1 1.1 %copy-done.2 = bf16[128,7168]{1,0:T(8,128)(2,1)} copy-done((bf16[128,7168]{1,0:T(8,128)(2,1)}, bf16[128,7168]{1,0:T(8,128)(2,1)S(1)}, u32[]{:S(2)}) %copy-start.2) | copy-done | bytes 1835032
  65.2 0.1 fusion.12
  65.3 0.7 fusion.30
  66.1 7.2 %fusion.32 = f32[128,1024]{1,0:T(8,128)S(1)} fusion(bf16[7168,1024]{1,0:T(8,128)(2,1)} %param.13, bf16[128,7296]{1,0:T(8,128)(2,1)S(1)} %copy-done.1), kind=kOutput, calls=%fused_computation.50 | convolution fusion | flops 1879048192 | bytes 17039360 | tf_op jit(solution)/shard_map/dot_general | solution.py:36
  73.4 1.4 %fusion.1 = f32[128,1024]{1,0:T(8,128)} fusion(f32[128,1024]{1,0:T(8,128)S(1)} %fusion.32, f32[128,64]{0,1:T(8,128)S(1)} %fusion.30, f32[16,8,8,128]{3,2,1,0:T(8,128)S(1)} %bitcast.52, f32[16,8,8,128]{3,2,1,0:T(8,128)S(1)} %bitcast.51, pred[1024]{0:T(1024)(128)(4,1)S(1)} %broadcast_bitcast_fusion, pred[1024]{0:T(1024)(128)(4,1)S(1)} %broadcast_bitcast_fusion.1, ...), kind=kOutput, calls=%fused_computation.2 | convolution fusion | flops 101318656 | bytes 2263044 | tf_op jit(solution)/shard_map/dot_general | solution.py:37
  74.8 0.0 reduce-scatter.2.cloned.1.call-update
  76.0 5.4 %all-gather = f32[512,64]{0,1:T(8,128)S(1)} all-gather(f32[128,64]{0,1:T(8,128)S(1)} %fusion.30), channel_id=2, replica_groups=mesh['dp'=8,'tensor'=4] {'tensor'}, dimensions={0}, use_global_device_ids=true | all-gather | bytes 163840 | tf_op jit(solution)/shard_map/all_gather | solution.py:52
  81.4 0.1 reduce_sum.9
  81.5 0.0 all-to-all-done
  81.5 1.6 %fusion.2 = f32[1,128,128]{2,1,0:T(8,128)S(1)} fusion(bf16[128,1024]{1,0:T(8,128)(2,1)S(1)} %bitcast.53, s32[]{:T(128)S(6)} %select_n.55, pred[]{:T(512)} %bitcast.7, bf16[128,7168]{1,0:T(8,128)(2,1)} %copy-done.2, s32[]{:T(128)S(6)} %select_n.49), kind=kOutput, calls=%fused_computation.4 | convolution fusion | flops 4210688 | bytes 131592 | tf_op jit(solution)/shard_map/dot_general | solution.py:67
  83.1 1.6 %fusion.3 = f32[1,128,128]{2,1,0:T(8,128)S(1)} fusion(bf16[128,1024]{1,0:T(8,128)(2,1)S(1)} %bitcast.54, s32[]{:T(128)S(6)} %select_n.52, pred[]{:T(512)} %bitcast.2, bf16[128,7168]{1,0:T(8,128)(2,1)} %copy-done.2, s32[]{:T(128)S(6)} %select_n.47), kind=kOutput, calls=%fused_computation.6 | convolution fusion | flops 4210688 | bytes 131592 | tf_op jit(solution)/shard_map/dot_general | solution.py:67
  84.7 0.7 maximum_bitcast_fusion
  85.4 1.0 fusion.37
  86.3 1.7 %fusion.10 = f32[7168,64]{0,1:T(8,128)} fusion(bf16[128,7296]{1,0:T(8,128)(2,1)S(1)} %copy-done.1), kind=kOutput, calls=%fused_computation.20 | convolution fusion | flops 117440512 | bytes 3702784 | tf_op jit(solution)/shard_map/dot_general | solution.py:60
  88.0 7.6 %reduce-scatter.2.cloned.1.call-done = f32[32,1024]{1,0:T(8,128)} async-done(((f32[128,1024]{1,0:T(8,128)}), f32[32,1024]{1,0:T(8,128)}) %reduce-scatter.2.cloned.1.call-update) | async-done | bytes 131088 | tf_op jit(solution)/shard_map/reduce_scatter | solution.py:51
  95.6 1.5 %convert_element_type.21 = bf16[32,1024]{1,0:T(8,128)(2,1)} convert(f32[32,1024]{1,0:T(8,128)} %reduce-scatter.2.cloned.1.call-done) | non-fusion elementwise | flops 32768 | bytes 196608 | tf_op jit(solution)/shard_map/convert_element_type | solution.py:51
  (10 shorter events, 0.1 us)
Async XLA Ops:
  7.2 1.4 %copy-start = (bf16[64,8192]{1,0:T(8,128)(2,1)S(1)}, bf16[64,8192]{1,0:T(8,128)(2,1)}, u32[]{:S(2)}) copy-start(bf16[64,8192]{1,0:T(8,128)(2,1)} %param.15) | copy-start | bytes 3145732
  7.2 3.6 %copy-start.3 = (bf16[16,8192]{1,0:T(8,128)(2,1)S(1)}, bf16[16,8192]{1,0:T(8,128)(2,1)}, u32[]{:S(2)}) copy-start(bf16[16,8192]{1,0:T(8,128)(2,1)} %param.12) | copy-start | bytes 786436
  7.2 11.6 %copy-start.5 = (s32[8,1,2]{0,2,1:T(2,128)S(1)}, s32[8,1,2]{0,2,1:T(2,128)}, u32[]{:S(2)}) copy-start(s32[8,1,2]{0,2,1:T(2,128)} %param.17) | copy-start | bytes 196
  7.2 11.6 %copy-start.6 = (s32[8,1,2]{0,2,1:T(2,128)S(1)}, s32[8,1,2]{0,2,1:T(2,128)}, u32[]{:S(2)}) copy-start(s32[8,1,2]{0,2,1:T(2,128)} %param.18) | copy-start | bytes 196
  7.2 13.5 %copy-start.8 = (s32[8,1]{0,1:T(1,128)S(1)}, s32[8,1]{0,1:T(1,128)}, u32[]{:S(2)}) copy-start(s32[8,1]{0,1:T(1,128)} %param.19) | copy-start | bytes 100
  7.2 54.9 %all-gather.3.cloned.1.call-start = ((), (), s32[]{:S(2)}) async-start(), calls=%async_computation.2 | async-start | bytes 2101248 | tf_op jit(solution)/shard_map/all_gather | solution.py:22
  11.5 70.0 %all-to-all-start = ((bf16[16,8,1024]{2,0,1:T(8,128)(2,1)}), bf16[16,8,1024]{2,0,1:T(8,128)(2,1)S(1)}, u32[]{:S(2)}, u32[]{:S(2)}) async-start(bf16[16,8,1024]{2,0,1:T(8,128)(2,1)} %bitcast.50), calls=%async_computation.1 | async-start | bytes 524288 | tf_op jit(solution)/shard_map/all_to_all | solution.py:26
  18.7 76.9 %reduce-scatter.2.cloned.1.call-start = ((), (), s32[]{:S(2)}) async-start(), calls=%async_computation.3 | async-start | bytes 655360 | tf_op jit(solution)/shard_map/reduce_scatter | solution.py:51
  25.7 38.3 %copy-start.4 = (bf16[1,1,2,128,128]{4,3,2,1,0:T(8,128)(2,1)S(1)}, bf16[1,1,2,128,128]{4,3,2,1,0:T(8,128)(2,1)}, u32[]{:S(2)}) copy-start(bf16[1,1,2,128,128]{4,3,2,1,0:T(8,128)(2,1)} %param.16) | copy-start | bytes 196612
  62.2 3.1 %copy-start.1 = (bf16[128,7296]{1,0:T(8,128)(2,1)S(1)}, bf16[128,7296]{1,0:T(8,128)(2,1)}, u32[]{:S(2)}) copy-start(bf16[128,7296]{1,0:T(8,128)(2,1)} %all-gather.3.cloned.1.call-done) | copy-start | bytes 5603332
  62.2 3.1 %copy-start.7 = (bf16[7168,64]{0,1:T(8,128)(2,1)S(1)}, bf16[7168,64]{0,1:T(8,128)(2,1)}, u32[]{:S(2)}) copy-start(bf16[7168,64]{0,1:T(8,128)(2,1)} %param.14) | copy-start | bytes 2752516
  63.9 1.2 %copy-start.2 = (bf16[128,7168]{1,0:T(8,128)(2,1)}, bf16[128,7168]{1,0:T(8,128)(2,1)S(1)}, u32[]{:S(2)}) copy-start(bf16[128,7168]{1,0:T(8,128)(2,1)S(1)} %slice.48) | copy-start | bytes 5505028
Sparse Core Ops, SparseCore 0:
  10.9 51.2 all-gather.2
  74.9 20.6 reduce-scatter.1

commit v2 on v1

--- a/solution.py
+++ b/solution.py
@@ -1,39 +1,233 @@
+import functools
+
 import jax
 import jax.numpy as jnp
 from jax import lax
+from jax.experimental import pallas as pl
+from jax.experimental.pallas import tpu as pltpu
 from jax.sharding import PartitionSpec as P
+
+MESH = pl.DeviceIdType.MESH
+F32, BF16 = jnp.float32, jnp.bfloat16
+WEIGHT_PARTS = 4
+
+
+def ring_place(index, n):
+    odd, pair = lax.rem(index, 2), lax.div(index, 2)
+    return (1 - odd) * pair + odd * (n - 1 - pair)
+
+
+def ring_index(place, n):
+    back = lax.div(place, n // 2)
+    return (1 - back) * 2 * place + back * (2 * (n - 1 - place) + 1)
+
+
+def gather_kernel(
+    n, gate, up, cot, w_hbm, a_hbm, b_hbm,
+    hid, cots, lows, total, low,
+    w, a, b, cl,
+    w_sem, ab_sem, ring_send, ring_recv, cot_send, cot_recv, cl_send, cl_recv,
+):
+    me = lax.axis_index("dp")
+    tok, quarter = gate.shape
+    width = cots.shape[1]
+    rank = b.shape[0]
+    part = quarter // WEIGHT_PARTS
+    loads = [pltpu.make_async_copy(b_hbm, b, ab_sem.at[0])]
+    loads += [
+        pltpu.make_async_copy(
+            w_hbm.at[pl.ds(i * part, part)], w.at[pl.ds(i * part, part)], w_sem.at[i]
+        )
+        for i in range(WEIGHT_PARTS)
+    ]
+    loads.append(pltpu.make_async_copy(a_hbm, a, ab_sem.at[1]))
+    for load in loads:
+        load.start()
+
+    barrier = pltpu.get_barrier_semaphore()
+
+    @pl.loop(1, n)
+    def _(d):
+        pl.semaphore_signal(
+            barrier, inc=1, device_id={"dp": lax.rem(me + d, n)}, device_id_type=MESH
+        )
+
+    def rows(index):
+        return pl.ds(pl.multiple_of(index * tok, tok), tok)
+
+    mine = rows(me)
+    half = quarter // 2
+    step = 512
+
+    @pl.loop(0, quarter // step)
+    def _(i):
+        at = pl.ds(pl.multiple_of(i * step, step), step)
+        g = gate[:, at].astype(F32)
+        hid[mine, at] = (g * jax.nn.sigmoid(g) * up[:, at].astype(F32)).astype(BF16)
+
+    pl.semaphore_wait(barrier, n - 1)
+
+    place = ring_place(me, n)
+    right = ring_index(lax.rem(place + 1, n), n)
+    left = ring_index(lax.rem(place + n - 1, n), n)
+    streams = ((0, 1, n // 2), (1, -1, n // 2), (1, 1, n // 2 - 1), (0, -1, n // 2 - 1))
+
+    def hop(k, s):
+        which, way, _ = streams[k]
+        slot = rows(ring_index(lax.rem(place - way * s + n, n), n))
+        ref = hid.at[slot, pl.ds(which * half, half)]
+        return pltpu.make_async_remote_copy(
+            src_ref=ref,
+            dst_ref=ref,
+            send_sem=ring_send.at[k, s],
+            recv_sem=ring_recv.at[k, s],
+            device_id={"dp": right if way > 0 else left},
+            device_id_type=MESH,
+        )
+
+    hops = {}
+
+    def start(k, s):
+        hops[k, s] = hop(k, s)
+        hops[k, s].start()
+
+    for k in range(4):
+        start(k, 0)
+
+    def cot_copy(d):
+        peer = lax.rem(me + d, n)
+        return pltpu.make_async_remote_copy(
+            src_ref=cot.at[:, pl.ds(pl.multiple_of(peer * width, width), width)],
+            dst_ref=cots.at[mine],
+            send_sem=cot_send.at[d],
+            recv_sem=cot_recv.at[d],
+            device_id={"dp": peer},
+            device_id_type=MESH,
+        )
+
+    def cl_copy(d):
+        return pltpu.make_async_remote_copy(
+            src_ref=cl,
+            dst_ref=lows.at[mine],
+            send_sem=cl_send.at[d],
+            recv_sem=cl_recv.at[d],
+            device_id={"dp": lax.rem(me + d, n)},
+            device_id_type=MESH,
+        )
+
+    @pl.loop(1, n)
+    def _(d):
+        cot_copy(d).start()
+
+    cots[mine] = cot[:, pl.ds(pl.multiple_of(me * width, width), width)]
+    loads[0].wait()
+    acc = jnp.zeros((tok, rank), F32)
+    deep = cot.shape[1] // 8
+    for i in range(8):
+        acc += lax.dot_general(
+            cot[:, i * deep : (i + 1) * deep],
+            b[:, i * deep : (i + 1) * deep],
+            (((1,), (1,)), ((), ())),
+            preferred_element_type=F32,
+        )
+    cl[...] = jnp.concatenate([acc, jnp.zeros((tok, cl.shape[1] - rank), F32)], axis=1).astype(BF16)
+    lows[mine] = cl[...]
+
+    @pl.loop(1, n)
+    def _(d):
+        cl_copy(d).start()
+
+    for s in range(n // 2):
+        for k in range(4):
+            if s < streams[k][2]:
+                hops[k, s].wait_recv()
+                if s + 1 < streams[k][2]:
+                    start(k, s + 1)
+
+    for load in loads[1:]:
+        load.wait()
+    total[...] = jnp.zeros_like(total)
+    low[...] = jnp.zeros_like(low)
+    tall = 1024
+
+    @pl.loop(0, quarter // tall)
+    def _(i):
+        at = pl.ds(pl.multiple_of(i * tall, tall), tall)
+        h = hid[:, at]
+        total[...] += jnp.dot(h, w[at], preferred_element_type=F32)
+        low[...] += jnp.dot(h, a[at], preferred_element_type=F32)
+
+    for one in hops.values():
+        one.wait_send()
+
+    @pl.loop(1, n)
+    def _(d):
+        cot_copy(d).wait()
+        cl_copy(d).wait()
+
+
+def gather_and_multiply(gate, up, cotangent, down_weight, factor_a, factor_b):
+    n = lax.axis_size("dp")
+    tok, quarter = gate.shape
+    width = down_weight.shape[1]
+    rank = factor_a.shape[1]
+    everyone = tok * n
+    vmem = pl.BlockSpec(memory_space=pltpu.VMEM)
+    anywhere = pl.BlockSpec(memory_space=pl.ANY)
+    dma = pltpu.SemaphoreType.DMA
+    return pl.pallas_call(
+        functools.partial(gather_kernel, n),
+        out_shape=(
+            jax.ShapeDtypeStruct((everyone, quarter), BF16),
+            jax.ShapeDtypeStruct((everyone, width), BF16),
+            jax.ShapeDtypeStruct((everyone, 128), BF16),
+            jax.ShapeDtypeStruct((everyone, width), F32),
+            jax.ShapeDtypeStruct((everyone, rank), F32),
+        ),
+        in_specs=[vmem, vmem, vmem, anywhere, anywhere, anywhere],
+        out_specs=[vmem] * 5,
+        scratch_shapes=[
+            pltpu.VMEM(down_weight.shape, BF16),
+            pltpu.VMEM(factor_a.shape, BF16),
+            pltpu.VMEM(factor_b.shape, BF16),
+            pltpu.VMEM((tok, 128), BF16),
+            dma((WEIGHT_PARTS,)),
+            dma((2,)),
+            dma((4, n // 2)),
+            dma((4, n // 2)),
+            dma((n,)),
+            dma((n,)),
+            dma((n,)),
+            dma((n,)),
+        ],
+        compiler_params=pltpu.CompilerParams(
+            collective_id=0, has_side_effects=True, vmem_limit_bytes=48 << 20
+        ),
+        name="gather_multiply",
+    )(gate, up, cotangent, down_weight, factor_a, factor_b)
 
 
 def shards(gate, up, cotangent, down_weight, factor_a, factor_b, blocks, slot_rows, slot_cols, counts):
     f32, bf16 = jnp.float32, jnp.bfloat16
     n_dp = lax.axis_size("dp")
     me = lax.axis_index("dp")
-    tok_local, quarter = gate.shape
+    tok_local = gate.shape[0]
     width = down_weight.shape[1]
     rank = factor_a.shape[1]
     side = blocks.shape[-1]
     slots = blocks.shape[2]
     per_col = width // side
-    hidden = (jax.nn.silu(gate.astype(f32)) * up.astype(f32)).astype(bf16)
-    cot_low = lax.dot_general(
-        cotangent, factor_b, (((1,), (1,)), ((), ())), preferred_element_type=f32
-    ).astype(bf16)
-    packed = jnp.concatenate([hidden, cot_low, jnp.zeros_like(cot_low)], axis=1)
-    packed_all = lax.all_gather(packed, "dp", axis=0, tiled=True)
-    hidden_all = packed_all[:, :quarter]
-    cot_low_all = packed_all[:, quarter : quarter + rank]
+    hidden_all, cot_cols, cot_low_all, total, low = gather_and_multiply(
+        gate, up, cotangent, down_weight, factor_a, factor_b
+    )
+    cot_low_all = cot_low_all[:, :rank]
     tok_all = tok_local * n_dp
-    cot_cols = lax.all_to_all(
-        cotangent.reshape(tok_local, n_dp, width), "dp", split_axis=1, concat_axis=0, tiled=True
-    ).reshape(tok_all, width)
     rows = lax.dynamic_index_in_dim(slot_rows[:, 0, :], me, 0, keepdims=False)
     cols = lax.dynamic_index_in_dim(slot_cols[:, 0, :], me, 0, keepdims=False)
     live = jnp.arange(slots, dtype=jnp.int32) < lax.dynamic_index_in_dim(
         counts[:, 0], me, 0, keepdims=False
     )
     b_window = lax.dynamic_slice_in_dim(factor_b, me * width, width, 1).astype(f32)
-    low = jnp.dot(hidden_all, factor_a, preferred_element_type=f32)
-    total = jnp.dot(hidden_all, down_weight, preferred_element_type=f32)
     total = total + jnp.dot(low, b_window, precision=lax.Precision.HIGHEST)
     owned_h = [
         lax.dynamic_slice_in_dim(hidden_all, rows[s] * side, side, 1) for s in range(slots)

time: 105 us -> 90.5 us (0.86)
  waiting for transfers between devices: 44.1 us -> 7.25 us
  Pallas kernels: 0 us -> 34.7 us
  matrix products: 16.8 us -> 8.72 us
  starting transfers between devices: 7.33 us -> 0.04 us
  local copies, waits for them, and re-layouts: 7.04 us -> 11.2 us
  other arithmetic: 6.64 us -> 5.41 us
    all_gather x1 -> x0, waiting for transfers between devices: 36.5 us -> none  [shards(): packed_all = lax.all_gather(packed, 'dp', axis=0, tiled=True)]
    pallas_call x0 -> x1, Pallas kernels: none -> 34.7 us  [gather_and_multiply(): pl.pallas_call(functools.partial(gather_kernel, n), out_shape=(jax.ShapeD...]
    dot_general x3 -> x0, matrix products: 9.29 us -> none  [the longest x1 7.23 us: shards(): total = jnp.dot(hidden_all, down_weight, preferred_element_type=f32)]
    all_to_all x1 -> x0, starting transfers between devices: 7.25 us -> none  [shards(): lax.all_to_all(cotangent.reshape(tok_local, n_dp, width), 'dp', split_axi...]
    unnamed x18 -> x17, local copies, waits for them, and re-layouts: 1.19 us -> 6.13 us
    slice x1 -> x0, local copies, waits for them, and re-layouts: 1.77 us -> none  [shards(): hidden_all = packed_all[:, :quarter]]
    broadcast_in_dim x4, local copies, waits for them, and re-layouts: 0.22 us -> 1.9 us  [shards(): jnp.where(pick[None, :, None], piece[:, None, :], 0.0)]
    convert_element_type x1 -> x0, other arithmetic: 1.27 us -> none  [shards(): hidden = (jax.nn.silu(gate.astype(f32)) * up.astype(f32)).astype(bf16)]
  transfers between devices with their start and end apart: 3 -> 1, of which waited for: 2 -> 1; matrix products, arithmetic and copies ran while one was open for 23% -> 7% of each run, Pallas kernels for 0% -> 0%
where the time goes in v2:
time: 90.5 us; the launch traced here: 89.9 us
  Pallas kernels  34.7 us (38%)
  between operations  16.7 us (18%)
  local copies, waits for them, and re-layouts  11.2 us (12%)
  matrix products  8.72 us (10%)
  waiting for transfers between devices  7.25 us (8%)
  blocking collectives  5.79 us (6%)
  other arithmetic  5.41 us (6%)
    pallas_call x1, Pallas kernels, gather_and_multiply(): pl.pallas_call(functools.partial(gather_kernel, n), out_shape=(jax.ShapeD...  34.7 us
    reduce_scatter x1, waiting for transfers between devices, shards(): lax.psum_scatter(total, 'tensor', scatter_dimension=0, tiled=True)  7.23 us
    unnamed x17, local copies, waits for them, and re-layouts  6.13 us
    all_gather x1, blocking collectives, shards(): low_parts = lax.all_gather(low, 'tensor', axis=0)  5.79 us
    dot_general x2, matrix products, shards(): lax.dot_general(owned_h[s], owned_c[s], (((0,), (0,)), ((), ())), preferr...  3.17 us
    and x2, other arithmetic, shards(): pick = (lanes == cols[s]) & live[s]  2.53 us
    broadcast_in_dim x4, local copies, waits for them, and re-layouts, shards(): jnp.where(pick[None, :, None], piece[:, None, :], 0.0)  1.9 us
  transfers between devices with their start and end apart: 1, of which 1 were waited for; matrix products, arithmetic and copies ran while one was open for 7% of the time, Pallas kernels for 0%

profile of v2, /device:TPU:0, one launch (start us, length us, event | category | flops | bytes accessed | tf_op | source)
XLA Modules:
  0.0 89.9 jit_solution(14460118171603083082)
XLA Ops:
  7.2 0.0 copy-start
  7.2 0.0 copy-start.1
  7.2 0.0 reduce-scatter.2.cloned.1.call-start
  7.2 0.8 constant_dynamic-slice_fusion
  8.1 0.5 fusion.25
  9.9 2.6 %copy.14.a_hbm = bf16[7168,64]{1,0:T(8,128)(2,1)} copy(bf16[7168,64]{0,1:T(8,128)(2,1)} %param.14) | data formatting | bytes 1835008 | tf_op args[4]
  12.5 0.0 copy-done.1
  12.5 0.0 copy-start.4
  12.5 0.9 %copy-done.4 = bf16[16,8192]{1,0:T(8,128)(2,1)S(1)} copy-done((bf16[16,8192]{1,0:T(8,128)(2,1)S(1)}, bf16[16,8192]{1,0:T(8,128)(2,1)}, u32[]{:S(2)}) %copy-start.4) | copy-done | bytes 262168
  13.5 0.0 copy-start.5
  13.5 0.9 %copy-done.5 = bf16[16,7168]{1,0:T(8,128)(2,1)S(1)} copy-done((bf16[16,7168]{1,0:T(8,128)(2,1)S(1)}, bf16[16,7168]{1,0:T(8,128)(2,1)}, u32[]{:S(2)}) %copy-start.5) | copy-done | bytes 229400
  14.4 0.0 copy-start.6
  14.4 0.9 %copy-done.6 = bf16[16,7168]{1,0:T(8,128)(2,1)S(1)} copy-done((bf16[16,7168]{1,0:T(8,128)(2,1)S(1)}, bf16[16,7168]{1,0:T(8,128)(2,1)}, u32[]{:S(2)}) %copy-start.6) | copy-done | bytes 229400
  15.3 0.0 copy-start.7
  15.3 34.7 %gather_multiply.1 = (bf16[128,7168]{1,0:T(8,128)(2,1)S(1)}, bf16[128,1024]{1,0:T(8,128)(2,1)S(1)}, bf16[128,128]{1,0:T(8,128)(2,1)S(1)}, f32[128,1024]{1,0:T(8,128)S(1)}, f32[128,64]{1,0:T(8,128)S(1)}) custom-call(bf16[16,7168]{1,0:T(8,128)(2,1)S(1)} %copy-done.5, bf16[16,7168]{1,0:T(8,128)(2,1)S(1)} %copy-done.6, bf16[16,8192]{1,0:T(8,128)(2,1)S(1)} %copy-done.4, ...), custom_call_target="tpu_custom_call" | custom-call | tf_op jit(solution)/shard_map/gather_multiply/pallas_call | solution.py:178
  50.1 0.0 copy-start.2
  50.1 0.7 copy-done.2
  50.8 0.0 copy-done.7
  50.8 0.8 fusion.5
  51.6 0.8 fusion.7
  52.3 0.0 copy-done
  52.3 0.6 constant_dynamic-slice_fusion.1
  52.9 0.6 iota_compare_fusion
  53.6 0.6 fusion.26
  54.2 0.6 fusion.24
  54.8 1.2 %compare_and_fusion = pred[8]{0:T(512)(128)(4,1)S(1)} fusion(pred[]{:T(512)} %bitcast.7, s32[]{:T(128)} %bitcast.6), kind=kLoop, calls=%fused_computation.33 | loop fusion | flops 16 | bytes 13 | tf_op jit(solution)/shard_map/and | solution.py:241
  56.0 0.1 broadcast_bitcast_fusion
  56.1 1.3 %compare_and_fusion.1 = pred[8]{0:T(512)(128)(4,1)S(1)} fusion(pred[]{:T(512)} %bitcast.2, s32[]{:T(128)} %bitcast), kind=kLoop, calls=%fused_computation.34 | loop fusion | flops 16 | bytes 13 | tf_op jit(solution)/shard_map/and | solution.py:241
  57.4 0.1 broadcast_bitcast_fusion.1
  57.5 0.9 broadcast_in_dim.64
  58.4 0.9 broadcast_in_dim.58
  59.2 1.3 %fusion.1 = f32[128,1024]{1,0:T(8,128)} fusion(f32[128,1024]{1,0:T(8,128)S(1)} %get-tuple-element.9, f32[128,64]{1,0:T(8,128)S(1)} %get-tuple-element.10, f32[16,8,8,128]{3,2,1,0:T(8,128)S(1)} %bitcast.38, f32[16,8,8,128]{3,2,1,0:T(8,128)S(1)} %bitcast.39, pred[1024]{0:T(1024)(128)(4,1)S(1)} %broadcast_bitcast_fusion, ...), kind=kOutput, calls=%fused_computation.2 | convolution fusion | flops 101318656 | bytes 2295812 | tf_op jit(solution)/shard_map/dot_general | solution.py:231
  60.5 0.0 copy-start.3
  60.5 0.0 reduce-scatter.2.cloned.1.call-update
  61.9 5.8 %all-gather = f32[512,64]{1,0:T(8,128)S(1)} all-gather(f32[128,64]{1,0:T(8,128)S(1)} %get-tuple-element.10), channel_id=2, replica_groups=mesh['dp'=8,'tensor'=4] {'tensor'}, dimensions={0}, use_global_device_ids=true | all-gather | bytes 163840 | tf_op jit(solution)/shard_map/all_gather | solution.py:246
  67.7 1.6 %fusion.2 = f32[1,128,128]{2,1,0:T(8,128)S(1)} fusion(bf16[128,1024]{1,0:T(8,128)(2,1)} %copy-done.2, s32[]{:T(128)S(6)} %select_n.55, pred[]{:T(512)} %bitcast.7, bf16[128,7168]{1,0:T(8,128)(2,1)S(1)} %get-tuple-element.11, s32[]{:T(128)S(6)} %select_n.49), kind=kOutput, calls=%fused_computation.4 | convolution fusion | flops 4210688 | bytes 131592 | tf_op jit(solution)/shard_map/dot_general | solution.py:261
  69.3 1.6 %fusion.3 = f32[1,128,128]{2,1,0:T(8,128)S(1)} fusion(bf16[128,1024]{1,0:T(8,128)(2,1)} %copy-done.2, s32[]{:T(128)S(6)} %select_n.52, pred[]{:T(512)} %bitcast.2, bf16[128,7168]{1,0:T(8,128)(2,1)S(1)} %get-tuple-element.11, s32[]{:T(128)S(6)} %select_n.47), kind=kOutput, calls=%fused_computation.6 | convolution fusion | flops 4210688 | bytes 131592 | tf_op jit(solution)/shard_map/dot_general | solution.py:261
  70.9 0.7 maximum_bitcast_fusion
  71.5 0.0 copy-done.3
  71.5 1.0 %fusion.27 = f32[64,1024]{1,0:T(8,128)} fusion(f32[128,64]{1,0:T(8,128)S(1)} %reduce_sum.9, bf16[128,1024]{1,0:T(8,128)(2,1)S(1)} %copy-done.3), kind=kOutput, calls=%fused_computation.41 | convolution fusion | flops 100663296 | bytes 557056 | tf_op jit(solution)/shard_map/dot_general | solution.py:248
  72.6 1.7 %fusion.11 = f32[7168,64]{0,1:T(8,128)} fusion(bf16[128,7168]{1,0:T(8,128)(2,1)S(1)} %get-tuple-element.11, bf16[128,128]{1,0:T(8,128)(2,1)S(1)} %get-tuple-element.12), kind=kOutput, calls=%fused_computation.17 | convolution fusion | flops 117440512 | bytes 3702784 | tf_op jit(solution)/shard_map/dot_general | solution.py:254
  74.2 7.2 %reduce-scatter.2.cloned.1.call-done = f32[32,1024]{1,0:T(8,128)} async-done(((f32[128,1024]{1,0:T(8,128)}), f32[32,1024]{1,0:T(8,128)}) %reduce-scatter.2.cloned.1.call-update) | async-done | bytes 131088 | tf_op jit(solution)/shard_map/reduce_scatter | solution.py:245
  81.5 1.5 %convert_element_type.2 = bf16[32,1024]{1,0:T(8,128)(2,1)} convert(f32[32,1024]{1,0:T(8,128)} %reduce-scatter.2.cloned.1.call-done) | non-fusion elementwise | flops 32768 | bytes 196608 | tf_op jit(solution)/shard_map/convert_element_type | solution.py:245
  (1 shorter events, 0.0 us)
Async XLA Ops:
  7.2 45.2 %copy-start = (s32[8,1]{0,1:T(1,128)S(1)}, s32[8,1]{0,1:T(1,128)}, u32[]{:S(2)}) copy-start(s32[8,1]{0,1:T(1,128)} %param.19) | copy-start | bytes 100
  7.2 5.3 %copy-start.1 = (bf16[64,8192]{1,0:T(8,128)(2,1)S(1)}, bf16[64,8192]{1,0:T(8,128)(2,1)}, u32[]{:S(2)}) copy-start(bf16[64,8192]{1,0:T(8,128)(2,1)} %b_hbm.1) | copy-start | bytes 3145732
  7.2 74.3 %reduce-scatter.2.cloned.1.call-start = ((), (), s32[]{:S(2)}) async-start(), calls=%async_computation.1 | async-start | bytes 655360 | tf_op jit(solution)/shard_map/reduce_scatter | solution.py:245
  12.5 1.0 %copy-start.4 = (bf16[16,8192]{1,0:T(8,128)(2,1)S(1)}, bf16[16,8192]{1,0:T(8,128)(2,1)}, u32[]{:S(2)}) copy-start(bf16[16,8192]{1,0:T(8,128)(2,1)} %cot.1) | copy-start | bytes 786436
  13.5 0.9 %copy-start.5 = (bf16[16,7168]{1,0:T(8,128)(2,1)S(1)}, bf16[16,7168]{1,0:T(8,128)(2,1)}, u32[]{:S(2)}) copy-start(bf16[16,7168]{1,0:T(8,128)(2,1)} %gate.1) | copy-start | bytes 688132
  14.4 0.9 %copy-start.6 = (bf16[16,7168]{1,0:T(8,128)(2,1)S(1)}, bf16[16,7168]{1,0:T(8,128)(2,1)}, u32[]{:S(2)}) copy-start(bf16[16,7168]{1,0:T(8,128)(2,1)} %up.1) | copy-start | bytes 688132
  15.3 35.5 %copy-start.7 = (bf16[1,1,2,128,128]{4,3,2,1,0:T(8,128)(2,1)S(1)}, bf16[1,1,2,128,128]{4,3,2,1,0:T(8,128)(2,1)}, u32[]{:S(2)}) copy-start(bf16[1,1,2,128,128]{4,3,2,1,0:T(8,128)(2,1)} %param.16) | copy-start | bytes 196612
  50.1 0.7 copy-start.2
  60.5 11.0 %copy-start.3 = (bf16[128,1024]{1,0:T(8,128)(2,1)S(1)}, bf16[128,1024]{1,0:T(8,128)(2,1)}, u32[]{:S(2)}) copy-start(bf16[128,1024]{1,0:T(8,128)(2,1)} %copy-done.2) | copy-start | bytes 786436
Sparse Core Ops, SparseCore 0:
  60.7 20.7 reduce-scatter.1

commit v3 on v2

--- a/solution.py
+++ b/solution.py
@@ -23,10 +23,11 @@
 
 
 def gather_kernel(
-    n, gate, up, cot, w_hbm, a_hbm, b_hbm,
-    hid, cots, lows, total, low,
-    w, a, b, cl,
+    n, n_tensor, gate, up, cot, w_hbm, a_hbm, b_hbm, blocks, slot_rows, slot_cols, counts,
+    hid, lows, mixed, grad_b, grad_blocks,
+    w, a, b, cl, cots, total, parts, low_parts,
     w_sem, ab_sem, ring_send, ring_recv, cot_send, cot_recv, cl_send, cl_recv,
+    low_send, low_recv, part_send, part_recv,
 ):
     me = lax.axis_index("dp")
     tok, quarter = gate.shape
@@ -52,6 +53,15 @@
             barrier, inc=1, device_id={"dp": lax.rem(me + d, n)}, device_id_type=MESH
         )
 
+    mine_t = lax.axis_index("tensor")
+    for d in range(1, n_tensor):
+        pl.semaphore_signal(
+            barrier,
+            inc=1,
+            device_id={"tensor": lax.rem(mine_t + d, n_tensor)},
+            device_id_type=MESH,
+        )
+
     def rows(index):
         return pl.ds(pl.multiple_of(index * tok, tok), tok)
 
@@ -65,7 +75,7 @@
         g = gate[:, at].astype(F32)
         hid[mine, at] = (g * jax.nn.sigmoid(g) * up[:, at].astype(F32)).astype(BF16)
 
-    pl.semaphore_wait(barrier, n - 1)
+    pl.semaphore_wait(barrier, n - 1 + n_tensor - 1)
 
     place = ring_place(me, n)
     right = ring_index(lax.rem(place + 1, n), n)
@@ -146,51 +156,148 @@
 
     for load in loads[1:]:
         load.wait()
-    total[...] = jnp.zeros_like(total)
-    low[...] = jnp.zeros_like(low)
     tall = 1024
-
-    @pl.loop(0, quarter // tall)
+    spread = quarter // tall
+    low = jnp.zeros((total.shape[0], rank), F32)
+    for i in range(spread):
+        at = slice(i * tall, (i + 1) * tall)
+        low += lax.dot_general(
+            hid[:, at], a[:, at], (((1,), (1,)), ((), ())), preferred_element_type=F32
+        )
+    low_parts[mine_t] = jnp.concatenate(
+        [low, jnp.zeros((low.shape[0], low_parts.shape[2] - rank), F32)], axis=1
+    )
+
+    def low_copy(d):
+        return pltpu.make_async_remote_copy(
+            src_ref=low_parts.at[mine_t],
+            dst_ref=low_parts.at[mine_t],
+            send_sem=low_send.at[d],
+            recv_sem=low_recv.at[d],
+            device_id={"tensor": lax.rem(mine_t + d, n_tensor)},
+            device_id_type=MESH,
+        )
+
+    share = mixed.shape[0]
+
+    def part_copy(d):
+        peer = lax.rem(mine_t + d, n_tensor)
+        return pltpu.make_async_remote_copy(
+            src_ref=total.at[pl.ds(pl.multiple_of(peer * share, share), share)],
+            dst_ref=parts.at[mine_t],
+            send_sem=part_send.at[d],
+            recv_sem=part_recv.at[d],
+            device_id={"tensor": peer},
+            device_id_type=MESH,
+        )
+
+    for d in range(1, n_tensor):
+        low_copy(d).start()
+
+    window = b[:, pl.ds(pl.multiple_of(me * width, width), width)].astype(F32)
+    total[...] = jnp.dot(low, window, precision=lax.Precision.HIGHEST, preferred_element_type=F32)
+    side = blocks.shape[-1]
+    slots = blocks.shape[0]
+
+    square = (hid.shape[0], side)
+
+    def owned(ref, block):
+        name = jnp.full(square, block, jnp.int32)
+
+        def look(r, kept):
+            here = ref[:, pl.ds(pl.multiple_of(r * side, side), side)].astype(F32)
+            return jnp.where(name == r, here, kept)
+
+        found = lax.fori_loop(0, ref.shape[1] // side, look, jnp.zeros(square, F32))
+        return found.astype(BF16)
+
+    live = jnp.full((8, side), counts[me, 0], jnp.int32)
+    held = [owned(hid, slot_rows[me, k]) for k in range(slots)]
+    for k in range(slots):
+        piece = jnp.dot(held[k], blocks[k], preferred_element_type=F32)
+        column = jnp.full((8, side), slot_cols[me, k], jnp.int32)
+        for c in range(width // side):
+            on = jnp.where((column == c) & (live > k), 1.0, 0.0)[:1]
+            total[:, c * side : (c + 1) * side] += piece * on
+
+    @pl.loop(0, spread)
     def _(i):
         at = pl.ds(pl.multiple_of(i * tall, tall), tall)
-        h = hid[:, at]
-        total[...] += jnp.dot(h, w[at], preferred_element_type=F32)
-        low[...] += jnp.dot(h, a[at], preferred_element_type=F32)
-
-    for one in hops.values():
-        one.wait_send()
+        total[...] += jnp.dot(hid[:, at], w[at], preferred_element_type=F32)
+
+    for d in range(1, n_tensor):
+        part_copy(d).start()
+    parts[mine_t] = total[pl.ds(pl.multiple_of(mine_t * share, share), share)]
 
     @pl.loop(1, n)
     def _(d):
         cot_copy(d).wait()
         cl_copy(d).wait()
 
-
-def gather_and_multiply(gate, up, cotangent, down_weight, factor_a, factor_b):
+    for k in range(slots):
+        block = lax.dot_general(
+            held[k],
+            owned(cots, slot_cols[me, k]),
+            (((0,), (0,)), ((), ())),
+            preferred_element_type=F32,
+        )
+        grad_blocks[k] = block * jnp.where(live > k, 1.0, 0.0)[:1]
+
+    for d in range(1, n_tensor):
+        low_copy(d).wait()
+    low_sum = low_parts[0]
+    for i in range(1, n_tensor):
+        low_sum += low_parts[i]
+    grad_b[...] = jnp.dot(
+        low_sum.T[:rank],
+        cots[...].astype(F32),
+        precision=lax.Precision.HIGHEST,
+        preferred_element_type=F32,
+    )
+
+    for d in range(1, n_tensor):
+        part_copy(d).wait()
+    whole = parts[0]
+    for i in range(1, n_tensor):
+        whole += parts[i]
+    mixed[...] = whole.astype(BF16)
+
+    for one in hops.values():
+        one.wait_send()
+
+
+def gather_and_multiply(
+    gate, up, cotangent, down_weight, factor_a, factor_b, blocks, slot_rows, slot_cols, counts
+):
+    n_tensor = lax.axis_size("tensor")
     n = lax.axis_size("dp")
     tok, quarter = gate.shape
     width = down_weight.shape[1]
-    rank = factor_a.shape[1]
+    rank = factor_a.shape[0]
     everyone = tok * n
     vmem = pl.BlockSpec(memory_space=pltpu.VMEM)
     anywhere = pl.BlockSpec(memory_space=pl.ANY)
     dma = pltpu.SemaphoreType.DMA
     return pl.pallas_call(
-        functools.partial(gather_kernel, n),
+        functools.partial(gather_kernel, n, n_tensor),
         out_shape=(
             jax.ShapeDtypeStruct((everyone, quarter), BF16),
-            jax.ShapeDtypeStruct((everyone, width), BF16),
             jax.ShapeDtypeStruct((everyone, 128), BF16),
-            jax.ShapeDtypeStruct((everyone, width), F32),
-            jax.ShapeDtypeStruct((everyone, rank), F32),
+            jax.ShapeDtypeStruct((everyone // n_tensor, width), BF16),
+            jax.ShapeDtypeStruct((rank, width), F32),
+            jax.ShapeDtypeStruct(blocks.shape, F32),
         ),
-        in_specs=[vmem, vmem, vmem, anywhere, anywhere, anywhere],
+        in_specs=[vmem] * 3 + [anywhere] * 3 + [vmem] + [pl.BlockSpec(memory_space=pltpu.SMEM)] * 3,
         out_specs=[vmem] * 5,
         scratch_shapes=[
             pltpu.VMEM(down_weight.shape, BF16),
             pltpu.VMEM(factor_a.shape, BF16),
             pltpu.VMEM(factor_b.shape, BF16),
             pltpu.VMEM((tok, 128), BF16),
+            pltpu.VMEM((everyone, width), BF16),
+            pltpu.VMEM((everyone, width), F32),
+            pltpu.VMEM((n_tensor, everyone // n_tensor, width), F32),
+            pltpu.VMEM((n_tensor, everyone, 128), F32),
             dma((WEIGHT_PARTS,)),
             dma((2,)),
             dma((4, n // 2)),
@@ -199,77 +306,41 @@
             dma((n,)),
             dma((n,)),
             dma((n,)),
+            dma((n_tensor,)),
+            dma((n_tensor,)),
+            dma((n_tensor,)),
+            dma((n_tensor,)),
         ],
         compiler_params=pltpu.CompilerParams(
             collective_id=0, has_side_effects=True, vmem_limit_bytes=48 << 20
         ),
         name="gather_multiply",
-    )(gate, up, cotangent, down_weight, factor_a, factor_b)
+    )(
+        gate, up, cotangent, down_weight, factor_a, factor_b, blocks, slot_rows, slot_cols, counts
+    )
 
 
 def shards(gate, up, cotangent, down_weight, factor_a, factor_b, blocks, slot_rows, slot_cols, counts):
-    f32, bf16 = jnp.float32, jnp.bfloat16
-    n_dp = lax.axis_size("dp")
-    me = lax.axis_index("dp")
-    tok_local = gate.shape[0]
-    width = down_weight.shape[1]
     rank = factor_a.shape[1]
-    side = blocks.shape[-1]
-    slots = blocks.shape[2]
-    per_col = width // side
-    hidden_all, cot_cols, cot_low_all, total, low = gather_and_multiply(
-        gate, up, cotangent, down_weight, factor_a, factor_b
-    )
-    cot_low_all = cot_low_all[:, :rank]
-    tok_all = tok_local * n_dp
-    rows = lax.dynamic_index_in_dim(slot_rows[:, 0, :], me, 0, keepdims=False)
-    cols = lax.dynamic_index_in_dim(slot_cols[:, 0, :], me, 0, keepdims=False)
-    live = jnp.arange(slots, dtype=jnp.int32) < lax.dynamic_index_in_dim(
-        counts[:, 0], me, 0, keepdims=False
-    )
-    b_window = lax.dynamic_slice_in_dim(factor_b, me * width, width, 1).astype(f32)
-    total = total + jnp.dot(low, b_window, precision=lax.Precision.HIGHEST)
-    owned_h = [
-        lax.dynamic_slice_in_dim(hidden_all, rows[s] * side, side, 1) for s in range(slots)
-    ]
-    owned_c = [
-        lax.dynamic_slice_in_dim(cot_cols, cols[s] * side, side, 1) for s in range(slots)
-    ]
-    lanes = jnp.arange(per_col, dtype=jnp.int32)
-    for s in range(slots):
-        piece = jnp.dot(owned_h[s], blocks[0, 0, s], preferred_element_type=f32)
-        pick = (lanes == cols[s]) & live[s]
-        total = total + jnp.where(
-            pick[None, :, None], piece[:, None, :], 0.0
-        ).reshape(tok_all, width)
-    mixed = lax.psum_scatter(total, "tensor", scatter_dimension=0, tiled=True).astype(bf16)
-    low_parts = lax.all_gather(low, "tensor", axis=0)
-    low_sum = jnp.sum(low_parts, axis=0)
-    grad_b = lax.dot_general(
-        low_sum,
-        cot_cols.astype(f32),
+    hidden_all, cot_low_all, mixed, grad_b, grad_blocks = gather_and_multiply(
+        gate,
+        up,
+        cotangent,
+        down_weight,
+        factor_a.T,
+        factor_b,
+        blocks[0, 0],
+        slot_rows[:, 0, :],
+        slot_cols[:, 0, :],
+        counts,
+    )
+    grad_a = lax.dot_general(
+        hidden_all,
+        cot_low_all[:, :rank],
         (((0,), (0,)), ((), ())),
-        precision=lax.Precision.HIGHEST,
-    )
-    grad_a = lax.dot_general(
-        hidden_all, cot_low_all, (((0,), (0,)), ((), ())), preferred_element_type=f32
-    )
-    grad_blocks = jnp.stack(
-        [
-            jnp.where(
-                live[s],
-                lax.dot_general(
-                    owned_h[s],
-                    owned_c[s],
-                    (((0,), (0,)), ((), ())),
-                    preferred_element_type=f32,
-                ),
-                0.0,
-            )
-            for s in range(slots)
-        ]
-    )[None, None]
-    return (mixed, grad_a, grad_b, grad_blocks)
+        preferred_element_type=F32,
+    )
+    return (mixed, grad_a, grad_b, grad_blocks[None, None])
 
 
 def solution(mesh):

time: 90.5 us -> 57.2 us (0.63)
  between operations: 16.7 us -> 0.65 us
  Pallas kernels: 34.7 us -> 43.5 us
  waiting for transfers between devices: 7.25 us -> 0 us
  matrix products: 8.72 us -> 1.68 us
  blocking collectives: 5.79 us -> 0 us
  other arithmetic: 5.41 us -> 0 us
    pallas_call x1, Pallas kernels: 34.7 us -> 43.5 us  [gather_and_multiply(): pl.pallas_call(functools.partial(gather_kernel, n, n_tensor), out_shape=(...]
    reduce_scatter x1 -> x0, waiting for transfers between devices: 7.23 us -> none  [shards(): lax.psum_scatter(total, 'tensor', scatter_dimension=0, tiled=True)]
    dot_general x7 -> x1, matrix products: 8.72 us -> 1.68 us  [shards(): lax.dot_general(hidden_all, cot_low_all[:, :rank], (((0,), (0,)), ((), ()...]
    all_gather x1 -> x0, blocking collectives: 5.79 us -> none  [shards(): low_parts = lax.all_gather(low, 'tensor', axis=0)]
    unnamed x17 -> x16, local copies, waits for them, and re-layouts: 6.13 us -> 8.78 us
    and x2 -> x0, other arithmetic: 2.53 us -> none  [shards(): pick = (lanes == cols[s]) & live[s]]
    broadcast_in_dim x4 -> x0, local copies, waits for them, and re-layouts: 1.9 us -> none  [shards(): jnp.where(pick[None, :, None], piece[:, None, :], 0.0)]
    slice x3 -> x0, local copies, waits for them, and re-layouts: 1.74 us -> none  [the longest x2 1.22 us: shards(): pick = (lanes == cols[s]) & live[s]]
  transfers between devices with their start and end apart: 1 -> 0, of which waited for: 1 -> 0; matrix products, arithmetic and copies ran while one was open for 7% -> 0% of each run, Pallas kernels for 0% -> 0%
where the time goes in v3:
time: 57.2 us; the launch traced here: 56.1 us
  Pallas kernels  43.5 us (76%)
  local copies, waits for them, and re-layouts  10.3 us (18%)
  matrix products  1.68 us (3%)
  between operations  0.65 us (1%)
    pallas_call x1, Pallas kernels, gather_and_multiply(): pl.pallas_call(functools.partial(gather_kernel, n, n_tensor), out_shape=(...  43.5 us
    unnamed x16, local copies, waits for them, and re-layouts  8.78 us
    dot_general x1, matrix products, shards(): lax.dot_general(hidden_all, cot_low_all[:, :rank], (((0,), (0,)), ((), ()...  1.68 us

profile of v3, /device:TPU:0, one launch (start us, length us, event | category | flops | bytes accessed | tf_op | source)
XLA Modules:
  0.0 56.1 jit_solution(15629164191022217648)
XLA Ops:
  0.6 0.8 %copy.14.slot_rows = s32[8,2]{1,0:T(8,128)S(1)} copy(s32[8,2]{0,1:T(2,128)} %bitcast.9) | data formatting | bytes 128 | tf_op jit(solution)/shard_map/squeeze | solution.py:333
  1.4 0.8 %copy.15.slot_cols = s32[8,2]{1,0:T(8,128)S(1)} copy(s32[8,2]{0,1:T(2,128)} %bitcast.10) | data formatting | bytes 128 | tf_op jit(solution)/shard_map/squeeze | solution.py:334
  2.1 0.7 %copy.16.counts = s32[8,1]{1,0:T(8,128)S(1)} copy(s32[8,1]{0,1:T(1,128)} %param.19) | data formatting | bytes 64 | tf_op args[9]
  2.9 0.0 copy-start
  2.9 1.2 %copy-done = bf16[64,8192]{1,0:T(8,128)(2,1)S(1)} copy-done((bf16[64,8192]{1,0:T(8,128)(2,1)S(1)}, bf16[64,8192]{1,0:T(8,128)(2,1)}, u32[]{:S(2)}) %copy-start) | copy-done | bytes 1048600
  4.1 0.0 copy-start.1
  4.1 1.2 %copy-done.1 = bf16[7168,64]{0,1:T(8,128)(2,1)S(1)} copy-done((bf16[7168,64]{0,1:T(8,128)(2,1)S(1)}, bf16[7168,64]{0,1:T(8,128)(2,1)}, u32[]{:S(2)}) %copy-start.1) | copy-done | bytes 917528
  5.3 0.0 copy-start.2
  5.3 0.9 %copy-done.2 = bf16[16,8192]{1,0:T(8,128)(2,1)S(1)} copy-done((bf16[16,8192]{1,0:T(8,128)(2,1)S(1)}, bf16[16,8192]{1,0:T(8,128)(2,1)}, u32[]{:S(2)}) %copy-start.2) | copy-done | bytes 262168
  6.2 0.0 copy-start.3
  6.2 0.9 %copy-done.3 = bf16[16,7168]{1,0:T(8,128)(2,1)S(1)} copy-done((bf16[16,7168]{1,0:T(8,128)(2,1)S(1)}, bf16[16,7168]{1,0:T(8,128)(2,1)}, u32[]{:S(2)}) %copy-start.3) | copy-done | bytes 229400
  7.2 0.0 copy-start.4
  7.2 0.9 %copy-done.4 = bf16[16,7168]{1,0:T(8,128)(2,1)S(1)} copy-done((bf16[16,7168]{1,0:T(8,128)(2,1)S(1)}, bf16[16,7168]{1,0:T(8,128)(2,1)}, u32[]{:S(2)}) %copy-start.4) | copy-done | bytes 229400
  8.1 0.0 copy-start.5
  8.1 0.8 %copy-done.5 = bf16[1,1,2,128,128]{4,3,2,1,0:T(8,128)(2,1)S(1)} copy-done((bf16[1,1,2,128,128]{4,3,2,1,0:T(8,128)(2,1)S(1)}, bf16[1,1,2,128,128]{4,3,2,1,0:T(8,128)(2,1)}, u32[]{:S(2)}) %copy-start.5) | copy-done | bytes 65560
  8.9 43.5 %gather_multiply.1 = (bf16[128,7168]{1,0:T(8,128)(2,1)S(1)}, bf16[128,128]{1,0:T(8,128)(2,1)S(1)}, bf16[32,1024]{1,0:T(8,128)(2,1)S(1)}, f32[64,1024]{1,0:T(8,128)S(1)}, f32[2,128,128]{2,1,0:T(8,128)S(1)}) custom-call(bf16[16,7168]{1,0:T(8,128)(2,1)S(1)} %copy-done.3, bf16[16,7168]{1,0:T(8,128)(2,1)S(1)} %copy-done.4, bf16[16,8192]{1,0:T(8,128)(2,1)S(1)} %copy-done.2, ...), custom_call_target="tpu_custom_call" | custom-call | tf_op jit(solution)/shard_map/gather_multiply/pallas_call | solution.py:281
  52.4 1.7 %fusion = f32[7168,64]{0,1:T(8,128)} fusion(bf16[128,7168]{1,0:T(8,128)(2,1)S(1)} %get-tuple-element.10, bf16[128,128]{1,0:T(8,128)(2,1)S(1)} %get-tuple-element.11), kind=kOutput, calls=%fused_computation | convolution fusion | flops 117440512 | bytes 3702784 | tf_op jit(solution)/shard_map/dot_general | solution.py:337
  54.1 0.6 %copy.20 = bf16[32,1024]{1,0:T(8,128)(2,1)} copy(bf16[32,1024]{1,0:T(8,128)(2,1)S(1)} %get-tuple-element.18) | data formatting | bytes 131072
  54.7 0.7 %copy.21 = f32[64,1024]{1,0:T(8,128)} copy(f32[64,1024]{1,0:T(8,128)S(1)} %get-tuple-element.20) | data formatting | bytes 524288
  55.4 0.7 %copy.22 = f32[1,1,2,128,128]{4,3,2,1,0:T(8,128)} copy(f32[1,1,2,128,128]{4,3,2,1,0:T(8,128)S(1)} %bitcast.7) | data formatting | bytes 262144
Async XLA Ops:
  2.9 1.2 %copy-start = (bf16[64,8192]{1,0:T(8,128)(2,1)S(1)}, bf16[64,8192]{1,0:T(8,128)(2,1)}, u32[]{:S(2)}) copy-start(bf16[64,8192]{1,0:T(8,128)(2,1)} %b_hbm.1) | copy-start | bytes 3145732
  4.1 1.2 %copy-start.1 = (bf16[7168,64]{0,1:T(8,128)(2,1)S(1)}, bf16[7168,64]{0,1:T(8,128)(2,1)}, u32[]{:S(2)}) copy-start(bf16[7168,64]{0,1:T(8,128)(2,1)} %param.14) | copy-start | bytes 2752516
  5.3 0.9 %copy-start.2 = (bf16[16,8192]{1,0:T(8,128)(2,1)S(1)}, bf16[16,8192]{1,0:T(8,128)(2,1)}, u32[]{:S(2)}) copy-start(bf16[16,8192]{1,0:T(8,128)(2,1)} %cot.1) | copy-start | bytes 786436
  6.2 0.9 %copy-start.3 = (bf16[16,7168]{1,0:T(8,128)(2,1)S(1)}, bf16[16,7168]{1,0:T(8,128)(2,1)}, u32[]{:S(2)}) copy-start(bf16[16,7168]{1,0:T(8,128)(2,1)} %gate.1) | copy-start | bytes 688132
  7.2 0.9 %copy-start.4 = (bf16[16,7168]{1,0:T(8,128)(2,1)S(1)}, bf16[16,7168]{1,0:T(8,128)(2,1)}, u32[]{:S(2)}) copy-start(bf16[16,7168]{1,0:T(8,128)(2,1)} %up.1) | copy-start | bytes 688132
  8.1 0.8 %copy-start.5 = (bf16[1,1,2,128,128]{4,3,2,1,0:T(8,128)(2,1)S(1)}, bf16[1,1,2,128,128]{4,3,2,1,0:T(8,128)(2,1)}, u32[]{:S(2)}) copy-start(bf16[1,1,2,128,128]{4,3,2,1,0:T(8,128)(2,1)} %param.16) | copy-start | bytes 196612

commit v4 on v3

--- a/solution.py
+++ b/solution.py
@@ -276,7 +276,7 @@
     rank = factor_a.shape[0]
     everyone = tok * n
     vmem = pl.BlockSpec(memory_space=pltpu.VMEM)
-    anywhere = pl.BlockSpec(memory_space=pl.ANY)
+    anywhere = pl.BlockSpec(memory_space=pltpu.HBM)
     dma = pltpu.SemaphoreType.DMA
     return pl.pallas_call(
         functools.partial(gather_kernel, n, n_tensor),
@@ -312,7 +312,7 @@
             dma((n_tensor,)),
         ],
         compiler_params=pltpu.CompilerParams(
-            collective_id=0, has_side_effects=True, vmem_limit_bytes=48 << 20
+            collective_id=0, has_side_effects=True, vmem_limit_bytes=60 << 20
         ),
         name="gather_multiply",
     )(

time: 57.2 us -> 55.9 us (0.977)
  local copies, waits for them, and re-layouts: 10.3 us -> 6.01 us
  matrix products: 1.68 us -> 3.23 us
  Pallas kernels: 43.5 us -> 45 us
    unnamed x16 -> x10, local copies, waits for them, and re-layouts: 8.78 us -> 3.32 us
    pallas_call x1, Pallas kernels: 43.5 us -> 45 us  [gather_and_multiply(): pl.pallas_call(functools.partial(gather_kernel, n, n_tensor), out_shape=(...]
    dot_general x1, matrix products: 1.68 us -> 3.23 us  [shards(): lax.dot_general(hidden_all, cot_low_all[:, :rank], (((0,), (0,)), ((), ()...]
    squeeze x1, local copies, waits for them, and re-layouts: 0.75 us -> 1.34 us  [shards(): slot_cols[:, 0, :]]
    squeeze x1, local copies, waits for them, and re-layouts: 0.75 us -> 1.35 us  [shards(): slot_rows[:, 0, :]]
where the time goes in v4:
time: 55.9 us; the launch traced here: 54.9 us
  Pallas kernels  45 us (81%)
  local copies, waits for them, and re-layouts  6.01 us (11%)
  matrix products  3.23 us (6%)
  between operations  0.67 us (1%)
    pallas_call x1, Pallas kernels, gather_and_multiply(): pl.pallas_call(functools.partial(gather_kernel, n, n_tensor), out_shape=(...  45 us
    unnamed x10, local copies, waits for them, and re-layouts  3.32 us
    dot_general x1, matrix products, shards(): lax.dot_general(hidden_all, cot_low_all[:, :rank], (((0,), (0,)), ((), ()...  3.23 us
    squeeze x1, local copies, waits for them, and re-layouts, shards(): slot_rows[:, 0, :]  1.35 us
    squeeze x1, local copies, waits for them, and re-layouts, shards(): slot_cols[:, 0, :]  1.34 us

profile of v4, /device:TPU:0, one launch (start us, length us, event | category | flops | bytes accessed | tf_op | source)
XLA Modules:
  0.0 54.9 jit_solution(13123855237971380291)
XLA Ops:
  0.6 1.3 %copy.14.slot_rows = s32[8,2]{1,0:T(8,128)} copy(s32[8,2]{0,1:T(2,128)} %bitcast.9) | data formatting | bytes 128 | tf_op jit(solution)/shard_map/squeeze | solution.py:333
  2.0 1.3 %copy.15.slot_cols = s32[8,2]{1,0:T(8,128)} copy(s32[8,2]{0,1:T(2,128)} %bitcast.10) | data formatting | bytes 128 | tf_op jit(solution)/shard_map/squeeze | solution.py:334
  3.3 1.3 %copy.16.counts = s32[8,1]{1,0:T(8,128)} copy(s32[8,1]{0,1:T(1,128)} %param.19) | data formatting | bytes 64 | tf_op args[9]
  4.6 45.0 %gather_multiply.1 = (bf16[128,7168]{1,0:T(8,128)(2,1)}, bf16[128,128]{1,0:T(8,128)(2,1)}, bf16[32,1024]{1,0:T(8,128)(2,1)}, f32[64,1024]{1,0:T(8,128)}, f32[2,128,128]{2,1,0:T(8,128)}) custom-call(bf16[16,7168]{1,0:T(8,128)(2,1)} %gate.1, bf16[16,7168]{1,0:T(8,128)(2,1)} %up.1, bf16[16,8192]{1,0:T(8,128)(2,1)} %cot.1, bf16[7168,1024]{1,0:T(8,128)(2,1)} %w_hbm.1, ...), custom_call_target="tpu_custom_call" | custom-call | tf_op jit(solution)/shard_map/gather_multiply/pallas_call | solution.py:281
  49.7 0.0 copy-start.2
  49.7 0.0 copy-start
  49.7 0.0 copy-start.1
  49.7 3.2 %fusion = f32[7168,64]{0,1:T(8,128)} fusion(bf16[128,7168]{1,0:T(8,128)(2,1)} %get-tuple-element.10, bf16[128,128]{1,0:T(8,128)(2,1)} %get-tuple-element.11), kind=kOutput, calls=%fused_computation | convolution fusion | flops 117440512 | bytes 3702784 | tf_op jit(solution)/shard_map/dot_general | solution.py:337
  52.9 0.0 copy-done.2
  53.0 0.6 %copy.20 = bf16[32,1024]{1,0:T(8,128)(2,1)} copy(bf16[32,1024]{1,0:T(8,128)(2,1)S(1)} %copy-done.2) | data formatting | bytes 131072
  53.6 0.0 copy-done
  53.6 0.7 %copy.21 = f32[64,1024]{1,0:T(8,128)} copy(f32[64,1024]{1,0:T(8,128)S(1)} %copy-done) | data formatting | bytes 524288
  54.3 0.0 copy-done.1
  54.3 0.7 %copy.22 = f32[1,1,2,128,128]{4,3,2,1,0:T(8,128)} copy(f32[1,1,2,128,128]{4,3,2,1,0:T(8,128)S(1)} %bitcast.7) | data formatting | bytes 262144
Async XLA Ops:
  49.7 3.3 %copy-start.2 = (bf16[32,1024]{1,0:T(8,128)(2,1)S(1)}, bf16[32,1024]{1,0:T(8,128)(2,1)}, u32[]{:S(2)}) copy-start(bf16[32,1024]{1,0:T(8,128)(2,1)} %get-tuple-element.18) | copy-start | bytes 196612
  49.7 3.9 %copy-start = (f32[64,1024]{1,0:T(8,128)S(1)}, f32[64,1024]{1,0:T(8,128)}, u32[]{:S(2)}) copy-start(f32[64,1024]{1,0:T(8,128)} %get-tuple-element.20) | copy-start | bytes 786436
  49.7 4.6 %copy-start.1 = (f32[2,128,128]{2,1,0:T(8,128)S(1)}, f32[2,128,128]{2,1,0:T(8,128)}, u32[]{:S(2)}) copy-start(f32[2,128,128]{2,1,0:T(8,128)} %get-tuple-element.13) | copy-start | bytes 393220
